TPU v7x, 32 devices: a whole 2x2x4 slice. The times are simulated.
32 devices in a mesh: fsdp: 8 (over y, x, core), seq: 4 (over z).
Axes of the slice: x: 2, y: 2, z: 4, core: 2. Of those that a mesh axis runs over, the one named last changes fastest.
Arguments:
- tokens: bfloat16 [64, 512, 768], P('fsdp', 'seq'), may hold values from -6 to 6
- lengths: int32 [64, 26], P('fsdp'), may hold values from 0 to 512, as said below
- cotangent: bfloat16 [64, 512, 768], P('fsdp', 'seq'), may hold values from -6 to 6
- project_weight: bfloat16 [768, 2304], P(('fsdp', 'seq')), may hold values from -0.21875 to 0.21875
- project_bias: bfloat16 [1536], P(('fsdp', 'seq')), may hold values from -3 to 3
- output_weight: bfloat16 [768, 768], P(('fsdp', 'seq')), may hold values from -0.875 to 0.875
- output_bias: bfloat16 [768], P(('fsdp', 'seq')), may hold values from -3 to 3
- first_gain: bfloat16 [768], P(('fsdp', 'seq')), may hold values from 0.099609375 to 1.8984375
- first_shift: bfloat16 [768], P(('fsdp', 'seq')), may hold values from -3 to 3
- expand_weight: bfloat16 [768, 3072], P(('fsdp', 'seq')), may hold values from -0.21875 to 0.21875
- expand_bias: bfloat16 [3072], P(('fsdp', 'seq')), may hold values from -3 to 3
- reduce_weight: bfloat16 [3072, 768], P(('fsdp', 'seq')), may hold values from -0.109375 to 0.109375
- reduce_bias: bfloat16 [768], P(('fsdp', 'seq')), may hold values from -3 to 3
- second_gain: bfloat16 [768], P(('fsdp', 'seq')), may hold values from 0.099609375 to 1.8984375
- second_shift: bfloat16 [768], P(('fsdp', 'seq')), may hold values from -3 to 3
Outputs:
- activations: bfloat16 [64, 512, 768], P('fsdp', 'seq')
- input_grad: float32 [64, 512, 768], P('fsdp', 'seq')
- project_grad: float32 [768, 2304], P(('fsdp', 'seq'))
- projbias_grad: float32 [1536], P(('fsdp', 'seq'))
- output_grad: float32 [768, 768], P(('fsdp', 'seq'))
- outbias_grad: float32 [768], P(('fsdp', 'seq'))
- firstgain_grad: float32 [768], P(('fsdp', 'seq'))
- firstshift_grad: float32 [768], P(('fsdp', 'seq'))
- expand_grad: float32 [768, 3072], P(('fsdp', 'seq'))
- expbias_grad: float32 [3072], P(('fsdp', 'seq'))
- reduce_grad: float32 [3072, 768], P(('fsdp', 'seq'))
- redbias_grad: float32 [768], P(('fsdp', 'seq'))
- secondgain_grad: float32 [768], P(('fsdp', 'seq'))
- secondshift_grad: float32 [768], P(('fsdp', 'seq'))
Inputs may be any that keep to these rules, and one draw needn't show every extreme that they name: Row r lists the lengths of the documents packed in order into sequence r; each row sums to 512; entries after the last document are 0; a document that is not its sequence's last has 20 to 200 tokens unless it fills the whole sequence.
All inputs are finite; a program needn't handle non-finite values.
Results may differ from a plain program's by a relative error of at most 0.013.
The roundings to bfloat16 on the way count: a program that leaves them out, or rounds other values in their place, can miss the bound.
Values may be sent and summed in bfloat16 or wider, within the bound.
A program may use at most 192 MiB of HBM per device.

v0:
```python
import math

import jax
import jax.numpy as jnp
from jax import lax
from jax.sharding import PartitionSpec as P

HEAD_DIM = 64


EPSILON = 1e-05


def layer_norm(values, gain, shift):
    centre = values - jnp.mean(values, axis=-1, keepdims=True)
    spread = jnp.mean(centre * centre, axis=-1, keepdims=True)
    return centre * lax.rsqrt(spread + EPSILON) * gain + shift


def gelu_exact(values):
    return jax.nn.gelu(values, approximate=False)


def heads_of(array):
    return array.reshape(array.shape[0], array.shape[1], -1, HEAD_DIM)


def grouped(array, size):
    return array.reshape((array.shape[0] // size, size) + array.shape[1:])


def scores_of(query_block, key_block, allowed_block):
    raw_scores = jnp.einsum(
        "sqhd,skhd->shqk",
        heads_of(query_block),
        heads_of(key_block),
        preferred_element_type=jnp.float32,
    ) * HEAD_DIM ** (-0.5)
    return jnp.where(allowed_block[:, None], raw_scores, -1e30)


def attend(pieces):
    query_block, key_block, value_block, allowed_block = pieces
    scores = scores_of(query_block, key_block, allowed_block)
    maxima = jnp.max(scores, axis=-1, keepdims=True)
    exponent = jnp.exp(scores - maxima)
    totals = jnp.sum(exponent, axis=-1, keepdims=True)
    probabilities = exponent / totals
    mixed_block = jnp.einsum(
        "shqk,skhd->sqhd",
        probabilities.astype(jnp.bfloat16),
        heads_of(value_block),
        preferred_element_type=jnp.float32,
    ).astype(jnp.bfloat16)
    return (mixed_block.reshape(query_block.shape), maxima + jnp.log(totals))


def attend_back(pieces):
    query_block, key_block, value_block, allowed_block, log_block, grad_block = pieces
    scale_now = HEAD_DIM ** (-0.5)
    scores = scores_of(query_block, key_block, allowed_block)
    probabilities = jnp.exp(scores - log_block)
    grad_heads = heads_of(grad_block)
    grad_probs = jnp.einsum(
        "sqhd,skhd->shqk", grad_heads, heads_of(value_block), preferred_element_type=jnp.float32
    )
    centred = jnp.sum(probabilities * grad_probs, axis=-1, keepdims=True)
    grad_scores = (probabilities * (grad_probs - centred)).astype(jnp.bfloat16)
    grad_query = (
        jnp.einsum(
            "shqk,skhd->sqhd", grad_scores, heads_of(key_block), preferred_element_type=jnp.float32
        )
        * scale_now
    )
    grad_key = (
        jnp.einsum(
            "shqk,sqhd->skhd",
            grad_scores,
            heads_of(query_block),
            preferred_element_type=jnp.float32,
        )
        * scale_now
    )
    grad_value = jnp.einsum(
        "shqk,sqhd->skhd",
        probabilities.astype(jnp.bfloat16),
        grad_heads,
        preferred_element_type=jnp.float32,
    )
    return (
        grad_query.reshape(query_block.shape),
        grad_key.reshape(key_block.shape),
        grad_value.reshape(key_block.shape),
    )


def shards(
    tokens,
    lengths,
    cotangent,
    project_weight,
    project_bias,
    output_weight,
    output_bias,
    first_gain,
    first_shift,
    expand_weight,
    expand_bias,
    reduce_weight,
    reduce_bias,
    second_gain,
    second_shift,
):
    (
        proj_full,
        pbias_full,
        out_full,
        obias_full,
        gain_one,
        shift_one,
        expand_full,
        ebias_full,
        reduce_full,
        rbias_full,
        gain_two,
        shift_two,
    ) = (
        lax.all_gather(project_weight, ("fsdp", "seq"), axis=0, tiled=True),
        lax.all_gather(project_bias, ("fsdp", "seq"), axis=0, tiled=True),
        lax.all_gather(output_weight, ("fsdp", "seq"), axis=0, tiled=True),
        lax.all_gather(output_bias, ("fsdp", "seq"), axis=0, tiled=True),
        lax.all_gather(first_gain, ("fsdp", "seq"), axis=0, tiled=True),
        lax.all_gather(first_shift, ("fsdp", "seq"), axis=0, tiled=True),
        lax.all_gather(expand_weight, ("fsdp", "seq"), axis=0, tiled=True),
        lax.all_gather(expand_bias, ("fsdp", "seq"), axis=0, tiled=True),
        lax.all_gather(reduce_weight, ("fsdp", "seq"), axis=0, tiled=True),
        lax.all_gather(reduce_bias, ("fsdp", "seq"), axis=0, tiled=True),
        lax.all_gather(second_gain, ("fsdp", "seq"), axis=0, tiled=True),
        lax.all_gather(second_shift, ("fsdp", "seq"), axis=0, tiled=True),
    )
    seqs_here, rows_here, model_width = tokens.shape
    length = rows_here * lax.axis_size("seq")
    positions = jnp.arange(length, dtype=jnp.int32)
    doc_ends = jnp.cumsum(lengths, axis=1)
    key_segments = jnp.sum(
        (positions[None, :, None] >= doc_ends[:, None, :]).astype(jnp.int32), axis=2
    )
    flattened = tokens.reshape(-1, model_width)
    qv_bias = pbias_full.astype(jnp.float32)
    full_bias = jnp.concatenate(
        [qv_bias[:model_width], jnp.zeros((model_width,), jnp.float32), qv_bias[model_width:]]
    )
    projected = (
        jnp.dot(flattened, proj_full, preferred_element_type=jnp.float32) + full_bias
    ).astype(jnp.bfloat16)
    queries = projected[:, :model_width].reshape(tokens.shape)
    keys_local = projected[:, model_width : 2 * model_width].reshape(tokens.shape)
    values_local = projected[:, 2 * model_width :].reshape(tokens.shape)
    keys_in, values_in = (
        lax.all_gather(keys_local, "seq", axis=1, tiled=True),
        lax.all_gather(values_local, "seq", axis=1, tiled=True),
    )
    query_segments = lax.dynamic_slice_in_dim(
        key_segments, lax.axis_index("seq") * rows_here, rows_here, 1
    )
    allowed = query_segments[:, :, None] == key_segments[:, None, :]
    group_size = math.gcd(seqs_here, max(1, 512 // rows_here))
    mixed_part, log_totals = lax.map(
        attend,
        (
            grouped(queries, group_size),
            grouped(keys_in, group_size),
            grouped(values_in, group_size),
            grouped(allowed, group_size),
        ),
    )
    mixed_part = mixed_part.reshape(queries.shape)
    mixed_flat = mixed_part.reshape(-1, model_width)
    attention = jnp.dot(
        mixed_flat, out_full, preferred_element_type=jnp.float32
    ) + obias_full.astype(jnp.float32)
    residual_one = flattened.astype(jnp.float32) + attention
    first_norm = layer_norm(
        residual_one, gain_one.astype(jnp.float32), shift_one.astype(jnp.float32)
    )
    first_low = first_norm.astype(jnp.bfloat16)
    inner_pre = jnp.dot(
        first_low, expand_full, preferred_element_type=jnp.float32
    ) + ebias_full.astype(jnp.float32)
    hidden = gelu_exact(inner_pre).astype(jnp.bfloat16)
    branch_out = jnp.dot(
        hidden, reduce_full, preferred_element_type=jnp.float32
    ) + rbias_full.astype(jnp.float32)
    residual_two = first_norm + branch_out
    result = layer_norm(residual_two, gain_two.astype(jnp.float32), shift_two.astype(jnp.float32))
    activations = result.astype(jnp.bfloat16).reshape(tokens.shape)
    (
        proj_full,
        pbias_full,
        out_full,
        obias_full,
        gain_one,
        shift_one,
        expand_full,
        ebias_full,
        reduce_full,
        rbias_full,
        gain_two,
        shift_two,
    ) = (
        lax.all_gather(project_weight, ("fsdp", "seq"), axis=0, tiled=True),
        lax.all_gather(project_bias, ("fsdp", "seq"), axis=0, tiled=True),
        lax.all_gather(output_weight, ("fsdp", "seq"), axis=0, tiled=True),
        lax.all_gather(output_bias, ("fsdp", "seq"), axis=0, tiled=True),
        lax.all_gather(first_gain, ("fsdp", "seq"), axis=0, tiled=True),
        lax.all_gather(first_shift, ("fsdp", "seq"), axis=0, tiled=True),
        lax.all_gather(expand_weight, ("fsdp", "seq"), axis=0, tiled=True),
        lax.all_gather(expand_bias, ("fsdp", "seq"), axis=0, tiled=True),
        lax.all_gather(reduce_weight, ("fsdp", "seq"), axis=0, tiled=True),
        lax.all_gather(reduce_bias, ("fsdp", "seq"), axis=0, tiled=True),
        lax.all_gather(second_gain, ("fsdp", "seq"), axis=0, tiled=True),
        lax.all_gather(second_shift, ("fsdp", "seq"), axis=0, tiled=True),
    )
    grad_result = cotangent.reshape(-1, model_width).astype(jnp.float32)
    norm_two_pull = jax.vjp(
        layer_norm, residual_two, gain_two.astype(jnp.float32), shift_two.astype(jnp.float32)
    )[1]
    grad_residual_two, grad_gain_two, grad_shift_two = norm_two_pull(grad_result)
    grad_branch = grad_residual_two.astype(jnp.bfloat16)
    grad_reduce = jnp.einsum("nf,nd->fd", hidden, grad_branch, preferred_element_type=jnp.float32)
    grad_rbias = jnp.sum(grad_branch.astype(jnp.float32), axis=0)
    grad_hidden = jnp.einsum(
        "nd,fd->nf", grad_branch, reduce_full, preferred_element_type=jnp.float32
    )
    grad_inner = jax.vjp(gelu_exact, inner_pre)[1](grad_hidden)[0].astype(jnp.bfloat16)
    grad_expand = jnp.einsum("nd,nf->df", first_low, grad_inner, preferred_element_type=jnp.float32)
    grad_ebias = jnp.sum(grad_inner.astype(jnp.float32), axis=0)
    grad_first = grad_residual_two + jnp.einsum(
        "nf,df->nd", grad_inner, expand_full, preferred_element_type=jnp.float32
    )
    norm_one_pull = jax.vjp(
        layer_norm, residual_one, gain_one.astype(jnp.float32), shift_one.astype(jnp.float32)
    )[1]
    grad_residual_one, grad_gain_one, grad_shift_one = norm_one_pull(grad_first)
    grad_attention = grad_residual_one.astype(jnp.bfloat16)
    grad_outw = jnp.einsum(
        "nd,ne->de", mixed_flat, grad_attention, preferred_element_type=jnp.float32
    )
    grad_obias = jnp.sum(grad_attention.astype(jnp.float32), axis=0)
    grad_mixed = (
        jnp.einsum("ne,de->nd", grad_attention, out_full, preferred_element_type=jnp.float32)
        .astype(jnp.bfloat16)
        .reshape(tokens.shape)
    )
    grad_queries, grad_keys_in, grad_values_in = lax.map(
        attend_back,
        (
            grouped(queries, group_size),
            grouped(keys_in, group_size),
            grouped(values_in, group_size),
            grouped(allowed, group_size),
            log_totals,
            grouped(grad_mixed, group_size),
        ),
    )
    grad_queries = grad_queries.reshape(queries.shape)
    grad_keys_in = grad_keys_in.reshape(keys_in.shape)
    grad_values_in = grad_values_in.reshape(keys_in.shape)
    grad_keys, grad_values = (
        lax.psum_scatter(
            grad_keys_in.astype(jnp.bfloat16), "seq", scatter_dimension=1, tiled=True
        ).astype(jnp.float32),
        lax.psum_scatter(
            grad_values_in.astype(jnp.bfloat16), "seq", scatter_dimension=1, tiled=True
        ).astype(jnp.float32),
    )
    grad_projected = jnp.concatenate(
        [
            grad_queries.reshape(-1, model_width),
            grad_keys.reshape(-1, model_width),
            grad_values.reshape(-1, model_width),
        ],
        axis=1,
    ).astype(jnp.bfloat16)
    grad_project = jnp.einsum(
        "nd,ne->de", flattened, grad_projected, preferred_element_type=jnp.float32
    )
    grad_column_sums = jnp.sum(grad_projected.astype(jnp.float32), axis=0)
    grad_pbias = jnp.concatenate(
        [grad_column_sums[:model_width], grad_column_sums[2 * model_width :]]
    )
    input_grad = (
        grad_residual_one
        + jnp.einsum("ne,de->nd", grad_projected, proj_full, preferred_element_type=jnp.float32)
    ).reshape(tokens.shape)
    (
        project_grad,
        projbias_grad,
        output_grad,
        outbias_grad,
        firstgain_grad,
        firstshift_grad,
        expand_grad,
        expbias_grad,
        reduce_grad,
        redbias_grad,
        secondgain_grad,
        secondshift_grad,
    ) = (
        lax.psum_scatter(grad_project, ("fsdp", "seq"), scatter_dimension=0, tiled=True),
        lax.psum_scatter(grad_pbias, ("fsdp", "seq"), scatter_dimension=0, tiled=True),
        lax.psum_scatter(grad_outw, ("fsdp", "seq"), scatter_dimension=0, tiled=True),
        lax.psum_scatter(grad_obias, ("fsdp", "seq"), scatter_dimension=0, tiled=True),
        lax.psum_scatter(grad_gain_one, ("fsdp", "seq"), scatter_dimension=0, tiled=True),
        lax.psum_scatter(grad_shift_one, ("fsdp", "seq"), scatter_dimension=0, tiled=True),
        lax.psum_scatter(grad_expand, ("fsdp", "seq"), scatter_dimension=0, tiled=True),
        lax.psum_scatter(grad_ebias, ("fsdp", "seq"), scatter_dimension=0, tiled=True),
        lax.psum_scatter(grad_reduce, ("fsdp", "seq"), scatter_dimension=0, tiled=True),
        lax.psum_scatter(grad_rbias, ("fsdp", "seq"), scatter_dimension=0, tiled=True),
        lax.psum_scatter(grad_gain_two, ("fsdp", "seq"), scatter_dimension=0, tiled=True),
        lax.psum_scatter(grad_shift_two, ("fsdp", "seq"), scatter_dimension=0, tiled=True),
    )
    return (
        activations,
        input_grad,
        project_grad,
        projbias_grad,
        output_grad,
        outbias_grad,
        firstgain_grad,
        firstshift_grad,
        expand_grad,
        expbias_grad,
        reduce_grad,
        redbias_grad,
        secondgain_grad,
        secondshift_grad,
    )


def solution(mesh):
    in_specs = (
        P("fsdp", "seq", None),
        P("fsdp", None),
        P("fsdp", "seq", None),
        P(("fsdp", "seq"), None),
        P(("fsdp", "seq")),
        P(("fsdp", "seq"), None),
        P(("fsdp", "seq")),
        P(("fsdp", "seq")),
        P(("fsdp", "seq")),
        P(("fsdp", "seq"), None),
        P(("fsdp", "seq")),
        P(("fsdp", "seq"), None),
        P(("fsdp", "seq")),
        P(("fsdp", "seq")),
        P(("fsdp", "seq")),
    )
    out_specs = (
        P("fsdp", "seq", None),
        P("fsdp", "seq", None),
        P(("fsdp", "seq"), None),
        P(("fsdp", "seq")),
        P(("fsdp", "seq"), None),
        P(("fsdp", "seq")),
        P(("fsdp", "seq")),
        P(("fsdp", "seq")),
        P(("fsdp", "seq"), None),
        P(("fsdp", "seq")),
        P(("fsdp", "seq"), None),
        P(("fsdp", "seq")),
        P(("fsdp", "seq")),
        P(("fsdp", "seq")),
    )
    return jax.shard_map(shards, mesh=mesh, in_specs=in_specs, out_specs=out_specs, check_vma=False)
```

profile of v0, /device:TPU:0, one launch (start us, length us, event | category | flops | bytes accessed | tf_op | source)
XLA Modules:
  0.0 1410.0 jit_solution(9618549883230010013)
XLA Ops:
  14.7 42.7 %all-reduce.17 = (bf16[1536]{0:T(1024)(128)(2,1)S(1)}, bf16[768]{0:T(1024)(128)(2,1)S(1)}, bf16[768]{0:T(1024)(128)(2,1)S(1)}, bf16[768]{0:T(1024)(128)(2,1)S(1)...) all-reduce(bf16[1536]{0:T(1024)(128)(2,1)S(1)} %dynamic-update-slic, ...), channel_id=1, replica_groups=mesh['fsdp'=8,'seq'=4] {'fsdp','seq'}, use_global_device_ids=true, to_apply=%add | all-reduce | flops 9216 | bytes 36864
  57.4 16.3 %all-gather.7.cloned.1.call-done = bf16[768,2304]{1,0:T(8,128)(2,1)} async-done(((bf16[24,2304]{1,0:T(8,128)(2,1)}), bf16[768,2304]{1,0:T(8,128)(2,1)}) %all-gather.7.cloned.1.call-update) | async-done | bytes 3538960 | tf_op jit(solution)/shard_map/all_gather | solution.py:128
  73.7 6.3 add_convert_fusion.1
  80.1 2.3 fusion.35
  92.9 103.8 %all-gather.9.cloned.1.call-done = bf16[8,512,768]{2,1,0:T(8,128)(2,1)} async-done(((bf16[8,128,768]{2,1,0:T(8,128)(2,1)}), bf16[8,512,768]{2,1,0:T(8,128)(2,1)}) %all-gather.9.cloned.1.call-update) | async-done | bytes 6291472 | tf_op jit(solution)/shard_map/all_gather | solution.py:161
  196.7 8.8 copy.55
  205.5 106.9 %all-gather.11.cloned.1.call-done = bf16[8,512,768]{2,1,0:T(8,128)(2,1)} async-done(((bf16[8,128,768]{2,1,0:T(8,128)(2,1)}), bf16[8,512,768]{2,1,0:T(8,128)(2,1)}) %all-gather.11.cloned.1.call-update) | async-done | bytes 6291472 | tf_op jit(solution)/shard_map/all_gather | solution.py:160
  312.4 8.7 copy.57
  321.1 33.4 %while.26 = (s32[]{:T(128)}, bf16[2,4,128,768]{3,2,1,0:T(8,128)(2,1)}, f32[2,4,12,128,1]{3,2,1,4,0:T(8,128)S(1)}, bf16[2,4,512,768]{2,3,1,0:T(8,128)(2,1)}, pred...) while((s32[]{:T(128)}, ...), condition=%wide.region_5.6_spmd, body=%wide.region_2.5_spmd.sunk | while | flops 843442176 | bytes 64447076 | solution.py:168
  321.1 3.3 constant_dynamic-slice_fusion.14
  325.4 2.7 fusion.96
  328.1 3.7 fusion.97
  331.9 4.7 fusion.98
  337.8 3.2 constant_dynamic-slice_fusion.14
  342.1 2.7 fusion.96
  344.8 3.7 fusion.97
  348.5 4.7 fusion.98
  354.5 12.8 all-gather.13.cloned.1.call-done
  367.4 3.8 fusion.38
  373.4 59.1 %all-gather.15.cloned.1.call-done = bf16[768,3072]{1,0:T(8,128)(2,1)} async-done(((bf16[24,3072]{1,0:T(8,128)(2,1)}), bf16[768,3072]{1,0:T(8,128)(2,1)}) %all-gather.15.cloned.1.call-update) | async-done | bytes 4718608 | tf_op jit(solution)/shard_map/all_gather | solution.py:134
  432.6 38.4 %multiply_convert_fusion.1 = (bf16[1024,3072]{1,0:T(8,128)(2,1)}, f32[1024,3072]{1,0:T(8,128)}, f32[1024,3072]{1,0:T(8,128)}) fusion(f32[3072]{0:T(1024)S(1)} %copy-done.33, bf16[768,3072]{1,0:T(8,128)(2,1)} %all-gather.15.cloned.1.call-done, f32[1024,768]{1,0:T(8,128)} %copy-done.5, f32[768]{0:T(1024)S(1)} %copy-done.24, f32[768]{0:T(1024)S(1)} %copy-done.22, ...), kind=kOutput, calls=%fused_computation.41 | convolution fusion | flops 5043388416 | bytes 39348224 | tf_op jit(solution)/shard_map/dot_general | solution.py:187
  471.0 26.6 %all-gather.17.cloned.1.call-done = bf16[3072,768]{1,0:T(8,128)(2,1)} async-done(((bf16[96,768]{1,0:T(8,128)(2,1)}), bf16[3072,768]{1,0:T(8,128)(2,1)}) %all-gather.17.cloned.1.call-update) | async-done | bytes 4718608 | tf_op jit(solution)/shard_map/all_gather | solution.py:136
  497.6 8.9 fusion.39
  508.8 2.8 fusion.33
  513.7 18.7 %convert_reduce_fusion = (f32[3072]{0:T(1024)}, bf16[1024,3072]{1,0:T(8,128)(2,1)}) fusion(f32[1024,3072]{1,0:T(8,128)} %get-tuple-element.299, bf16[1024,768]{1,0:T(8,128)(2,1)} %get-tuple-element.291, bf16[3072,768]{1,0:T(8,128)(2,1)} %all-gather.17.cloned.1.call-done, f32[1024,3072]{1,0:T(8,128)} %get-tuple-element.318, f32[3072]{0:T(1024)S(1)} %copy-done.33), kind=kOutput, calls=%fused_computation.39 | convolution fusion | flops 4885312512 | bytes 37773312 | tf_op jit(solution)/shard_map/nd,fd->nf/dot_general | solution.py:232
  532.4 10.1 multiply_reduce_fusion.1
  546.1 2.6 convolution_convert_fusion
  548.7 108.3 %while.27 = (s32[]{:T(128)}, bf16[2,4,128,768]{3,2,1,0:T(8,128)(2,1)}, bf16[2,4,512,768]{2,3,1,0:T(8,128)(2,1)}, bf16[2,4,512,768]{2,3,1,0:T(8,128)(2,1)}, bf16[...) while((s32[]{:T(128)}, ...), condition=%wide.region_16.17_spmd, body=%wide.region_14.16_spmd.sunk | while | flops 2064377856 | bytes 208315760 | solution.py:255
  548.9 2.2 constant_dynamic-slice_fusion.16
  551.4 6.4 fusion.109
  559.7 2.3 copy.93
  562.0 2.2 constant_dynamic-slice_fusion.19
  564.2 11.5 multiply_reduce_fusion.6
  575.8 7.0 multiply_convert_fusion.3
  582.8 2.7 broadcast_multiply_fusion.4
  585.5 6.0 fusion.110
  591.5 5.9 constant_dynamic-update-slice_fusion.9
  597.4 3.3 convolution_multiply_fusion.2
  603.0 2.2 constant_dynamic-slice_fusion.16
  605.4 6.4 fusion.109
  613.8 2.3 copy.93
  616.1 2.2 constant_dynamic-slice_fusion.19
  618.3 11.5 multiply_reduce_fusion.6
  629.8 7.0 multiply_convert_fusion.3
  636.8 2.7 broadcast_multiply_fusion.4
  639.5 6.0 fusion.110
  645.5 5.8 constant_dynamic-update-slice_fusion.9
  651.4 3.3 convolution_multiply_fusion.2
  657.0 8.7 copy.63
  665.8 8.7 copy.64
  674.9 4.9 fusion.41
  680.0 10.7 fusion.28
  692.1 10.2 fusion.42
  702.4 73.1 %reduce-scatter.9.cloned.1.call-done = bf16[8,128,768]{2,1,0:T(8,128)(2,1)} async-done(((bf16[8,512,768]{2,1,0:T(8,128)(2,1)}), bf16[8,128,768]{2,1,0:T(8,128)(2,1)}) %reduce-scatter.9.cloned.1.call-update) | async-done | bytes 1572880 | tf_op jit(solution)/shard_map/reduce_scatter | solution.py:270
  775.5 113.6 %reduce-scatter.11.cloned.1.call-done = bf16[8,128,768]{2,1,0:T(8,128)(2,1)} async-done(((bf16[8,512,768]{2,1,0:T(8,128)(2,1)}), bf16[8,128,768]{2,1,0:T(8,128)(2,1)}) %reduce-scatter.11.cloned.1.call-update) | async-done | bytes 1572880 | tf_op jit(solution)/shard_map/reduce_scatter | solution.py:273
  889.1 8.6 convolution_bitcast_fusion
  897.7 8.1 copy.66
  907.5 3.0 convert_reduce_fusion.1
  910.6 42.1 %all-reduce.16 = (f32[1536]{0:T(1024)S(1)}, f32[768]{0:T(1024)S(1)}, f32[768]{0:T(1024)S(1)}, f32[768]{0:T(1024)S(1)}, f32[3072]{0:T(1024)S(1)}, /*index=5*/f32[...) all-reduce(f32[1536]{0:T(1024)S(1)} %pad_maximum_fusion.2, ...), channel_id=5, replica_groups=mesh['fsdp'=8,'seq'=4] {'fsdp','seq'}, use_global_device_ids=true, to_apply=%region_21.22.clone | all-reduce | flops 9216 | bytes 73728
  957.3 9.0 add_add_fusion.4
  966.3 28.6 %reduce-scatter.13.cloned.1.call-done = f32[24,768]{1,0:T(8,128)} async-done(((f32[768,768]{1,0:T(8,128)}), f32[24,768]{1,0:T(8,128)}) %reduce-scatter.13.cloned.1.call-update) | async-done | bytes 73744 | tf_op jit(solution)/shard_map/reduce_scatter | solution.py:312
  994.9 141.8 %reduce-scatter.15.cloned.1.call-done = f32[24,3072]{1,0:T(8,128)} async-done(((f32[768,3072]{1,0:T(8,128)}), f32[24,3072]{1,0:T(8,128)}) %reduce-scatter.15.cloned.1.call-update) | async-done | bytes 294928 | tf_op jit(solution)/shard_map/reduce_scatter | solution.py:316
  1136.7 141.1 %reduce-scatter.17.cloned.1.call-done = f32[96,768]{1,0:T(8,128)} async-done(((f32[3072,768]{1,0:T(8,128)}), f32[96,768]{1,0:T(8,128)}) %reduce-scatter.17.cloned.1.call-update) | async-done | bytes 294928 | tf_op jit(solution)/shard_map/reduce_scatter | solution.py:318
  1277.8 125.2 %reduce-scatter.19.cloned.1.call-done = f32[24,2304]{1,0:T(8,128)} async-done(((f32[768,2304]{1,0:T(8,128)}), f32[24,2304]{1,0:T(8,128)}) %reduce-scatter.19.cloned.1.call-update) | async-done | bytes 221200
  (217 shorter events, 50.0 us)
Async XLA Ops:
  7.2 66.6 %all-gather.7.cloned.1.call-start = ((), (), s32[]{:S(2)}) async-start(), calls=%async_computation.6 | async-start | bytes 3649536 | tf_op jit(solution)/shard_map/all_gather | solution.py:128
  7.9 188.8 %all-gather.9.cloned.1.call-start = ((), (), s32[]{:S(2)}) async-start(), calls=%async_computation.7 | async-start | bytes 7864320 | tf_op jit(solution)/shard_map/all_gather | solution.py:161
  80.1 5.1 copy-start.37
  82.4 230.0 %all-gather.11.cloned.1.call-start = ((), (), s32[]{:S(2)}) async-start(), calls=%async_computation.8 | async-start | bytes 7864320 | tf_op jit(solution)/shard_map/all_gather | solution.py:160
  83.1 284.3 %all-gather.13.cloned.1.call-start = ((), (), s32[]{:S(2)}) async-start(), calls=%async_computation.9 | async-start | bytes 1216512 | tf_op jit(solution)/shard_map/all_gather | solution.py:130
  83.7 348.9 %all-gather.15.cloned.1.call-start = ((), (), s32[]{:S(2)}) async-start(), calls=%async_computation.10 | async-start | bytes 4866048 | tf_op jit(solution)/shard_map/all_gather | solution.py:134
  84.3 413.3 %all-gather.17.cloned.1.call-start = ((), (), s32[]{:S(2)}) async-start(), calls=%async_computation.11 | async-start | bytes 4866048 | tf_op jit(solution)/shard_map/all_gather | solution.py:136
  84.8 690.6 %reduce-scatter.9.cloned.1.call-start = ((), (), s32[]{:S(2)}) async-start(), calls=%async_computation.12 | async-start | bytes 7864320 | tf_op jit(solution)/shard_map/reduce_scatter | solution.py:270
  321.1 46.3 %copy-start.36 = (f32[768]{0:T(1024)S(1)}, f32[768]{0:T(1024)}, u32[]{:S(2)}) copy-start(f32[768]{0:T(1024)} %convert_element_type.111) | copy-start | bytes 9220
  354.5 16.7 %copy-start.3 = (bf16[2,4,128,768]{2,3,1,0:T(8,128)(2,1)}, bf16[2,4,128,768]{2,3,1,0:T(8,128)(2,1)S(1)}, u32[]{:S(2)}) copy-start(bf16[2,4,128,768]{2,3,1,0:T(8,128)(2,1)S(1)} %get-tuple-element.515) | copy-start | bytes 4718596
  354.5 16.7 %copy-start.16 = (f32[2,4,12,128,1]{3,2,1,4,0:T(8,128)}, f32[2,4,12,128,1]{3,2,1,4,0:T(8,128)S(1)}, u32[]{:S(2)}) copy-start(f32[2,4,12,128,1]{3,2,1,4,0:T(8,128)S(1)} %get-tuple-element.475) | copy-start | bytes 147460
  367.4 65.2 %copy-start.22 = (f32[768]{0:T(1024)S(1)}, f32[768]{0:T(1024)}, u32[]{:S(2)}) copy-start(f32[768]{0:T(1024)} %convert_element_type.112) | copy-start | bytes 9220
  367.4 65.2 %copy-start.24 = (f32[768]{0:T(1024)S(1)}, f32[768]{0:T(1024)}, u32[]{:S(2)}) copy-start(f32[768]{0:T(1024)} %convert_element_type.113) | copy-start | bytes 9220
  367.4 65.2 %copy-start.33 = (f32[3072]{0:T(1024)S(1)}, f32[3072]{0:T(1024)}, u32[]{:S(2)}) copy-start(f32[3072]{0:T(1024)} %convert_element_type.115) | copy-start | bytes 36868
  371.2 1.7 copy-start.5
  371.2 171.3 %copy-start.18 = (f32[1024]{0:T(1024)}, f32[1024]{0:T(1024)S(1)}, u32[]{:S(2)}) copy-start(f32[1024]{0:T(1024)S(1)} %broadcast_multiply_fusion.2) | copy-start | bytes 12292
  373.4 169.1 %copy-start.20 = (f32[1024]{0:T(1024)}, f32[1024]{0:T(1024)S(1)}, u32[]{:S(2)}) copy-start(f32[1024]{0:T(1024)S(1)} %fusion.26) | copy-start | bytes 12292
  373.4 124.1 %copy-start.6 = (f32[1024,768]{1,0:T(8,128)S(1)}, f32[1024,768]{1,0:T(8,128)}, u32[]{:S(2)}) copy-start(f32[1024,768]{1,0:T(8,128)} %copy-done.5) | copy-start | bytes 9437188
  373.4 124.1 %copy-start.35 = (f32[768]{0:T(1024)S(1)}, f32[768]{0:T(1024)}, u32[]{:S(2)}) copy-start(f32[768]{0:T(1024)} %convert_element_type.117) | copy-start | bytes 9220
  497.6 9.5 copy-start.8
  497.6 9.5 copy-start.26
  506.5 2.3 copy-start.29
  544.0 4.7 copy-start.10
  544.0 2.1 copy-start.41
  544.0 4.7 copy-start.27
  544.9 3.8 copy-start.15
  546.1 2.6 copy-start.17
  548.9 2.4 copy-start.4
  551.3 6.4 copy-start
  551.4 7.4 copy-start.12
  562.0 2.2 copy-start.2
  564.2 11.6 slice-start
  564.2 11.6 slice-start.1
  564.2 11.6 slice-start.2
  575.8 7.0 copy-start.1
  603.0 2.4 copy-start.4
  605.4 6.4 copy-start
  605.4 7.4 copy-start.12
  616.1 2.2 copy-start.2
  618.2 11.6 slice-start
  618.3 11.6 slice-start.1
  618.3 11.6 slice-start.2
  629.8 7.0 copy-start.1
  665.8 223.3 %reduce-scatter.11.cloned.1.call-start = ((), (), s32[]{:S(2)}) async-start(), calls=%async_computation.13 | async-start | bytes 7864320 | tf_op jit(solution)/shard_map/reduce_scatter | solution.py:273
  674.5 5.4 copy-start.7
  674.6 5.4 copy-start.19
  674.6 5.4 copy-start.21
  674.6 5.4 copy-start.23
  674.6 5.4 copy-start.25
  674.6 320.3 %reduce-scatter.13.cloned.1.call-start = ((), (), s32[]{:S(2)}) async-start(), calls=%async_computation.14 | async-start | bytes 2433024 | tf_op jit(solution)/shard_map/reduce_scatter | solution.py:312
  679.9 456.8 %reduce-scatter.15.cloned.1.call-start = ((), (), s32[]{:S(2)}) async-start(), calls=%async_computation.15 | async-start | bytes 9732096 | tf_op jit(solution)/shard_map/reduce_scatter | solution.py:316
  690.6 1.5 copy-start.14
  690.7 587.1 %reduce-scatter.17.cloned.1.call-start = ((), (), s32[]{:S(2)}) async-start(), calls=%async_computation.16 | async-start | bytes 9732096 | tf_op jit(solution)/shard_map/reduce_scatter | solution.py:318
  702.3 186.8 %copy-start.13 = (bf16[2,4,128,768]{3,2,1,0:T(8,128)(2,1)S(1)}, bf16[2,4,128,768]{3,2,1,0:T(8,128)(2,1)}, u32[]{:S(2)}) copy-start(bf16[2,4,128,768]{3,2,1,0:T(8,128)(2,1)} %get-tuple-element.108) | copy-start | bytes 4718596
  702.3 186.8 %copy-start.40 = (bf16[8,128,768]{2,1,0:T(8,128)(2,1)S(1)}, bf16[8,128,768]{2,1,0:T(8,128)(2,1)}, u32[]{:S(2)}) copy-start(bf16[8,128,768]{2,1,0:T(8,128)(2,1)} %param.19) | copy-start | bytes 4718596
  702.3 700.7 %reduce-scatter.19.cloned.1.call-start = ((), (), s32[]{:S(2)}) async-start(), calls=%async_computation.17 | async-start | bytes 7299072
  905.8 4.7 copy-start.30
  905.8 4.7 copy-start.31
  905.8 4.7 copy-start.32
  905.8 4.7 copy-start.34
  905.8 4.7 copy-start.38
  905.9 4.7 copy-start.39
  905.9 51.5 %copy-start.28 = (f32[1024]{0:T(1024)S(1)}, f32[1024]{0:T(1024)}, u32[]{:S(2)}) copy-start(f32[1024]{0:T(1024)} %copy-done.27) | copy-start | bytes 12292
  907.5 49.9 %copy-start.11 = (f32[1024,768]{1,0:T(8,128)S(1)}, f32[1024,768]{1,0:T(8,128)}, u32[]{:S(2)}) copy-start(f32[1024,768]{1,0:T(8,128)} %copy-done.10) | copy-start | bytes 9437188
  (1 other events, 1.4 us)
Sparse Core Ops, SparseCore 0:
  10.8 62.8 all-gather.6
  82.5 114.1 all-gather.8
  198.8 113.5 all-gather.10
  315.1 52.2 all-gather.12
  370.0 62.4 all-gather.14
  435.2 62.3 all-gather.16
  665.9 109.5 reduce-scatter.8
  777.8 111.2 reduce-scatter.10
  895.0 99.8 reduce-scatter.12
  1002.2 134.4 reduce-scatter.14
  1143.2 134.5 reduce-scatter.16
  1284.9 118.1 reduce-scatter.18
where the time goes:
time: 1420 us; the launch traced here: 1410 us
  waiting for transfers between devices  952 us (67%)
  matrix products  207 us (15%)
  local copies, waits for them, and re-layouts  110 us (8%)
  blocking collectives  84.8 us (6%)
  other arithmetic  40.3 us (3%)
  between operations  14.9 us (1%)
    reduce_scatter x1, waiting for transfers between devices, shards(): lax.psum_scatter(grad_expand, ('fsdp', 'seq'), scatter_dimension=0, tiled...  142 us
    reduce_scatter x1, waiting for transfers between devices, shards(): lax.psum_scatter(grad_reduce, ('fsdp', 'seq'), scatter_dimension=0, tiled...  141 us
    unnamed x13, waiting for transfers between devices  128 us
    reduce_scatter x1, waiting for transfers between devices, shards(): lax.psum_scatter(grad_values_in.astype(jnp.bfloat16), 'seq', scatter_dime...  114 us
    all_gather x1, waiting for transfers between devices, shards(): lax.all_gather(keys_local, 'seq', axis=1, tiled=True)  107 us
    all_gather x1, waiting for transfers between devices, shards(): lax.all_gather(values_local, 'seq', axis=1, tiled=True)  104 us
    unnamed x2, blocking collectives  84.8 us
    reduce_scatter x1, waiting for transfers between devices, shards(): lax.psum_scatter(grad_keys_in.astype(jnp.bfloat16), 'seq', scatter_dimens...  73.1 us
  transfers between devices with their start and end apart: 12, of which 12 were waited for; matrix products, arithmetic and copies ran while one was open for 12% of the time, Pallas kernels for 0%

commit v1 on v0

v1 whole, which is shorter than its diff:
```python
import functools

import jax
import jax.numpy as jnp
from jax import lax
from jax.experimental import pallas as pl
from jax.experimental.pallas import tpu as pltpu
from jax.sharding import PartitionSpec as P

HEAD_DIM = 64
PAIR = 2 * HEAD_DIM
PAD = 128
VMEM_BYTES = 40 * 1024 * 1024


EPSILON = 1e-05


def layer_norm(values, gain, shift):
    centre = values - jnp.mean(values, axis=-1, keepdims=True)
    spread = jnp.mean(centre * centre, axis=-1, keepdims=True)
    return centre * lax.rsqrt(spread + EPSILON) * gain + shift


def normal_cdf(values):
    return 0.5 + 0.5 * lax.erf(values * 0.5**0.5)


def gelu_slope(values):
    density = jnp.exp(values * values * -0.5) * 0.3989422804014327
    return normal_cdf(values) + values * density


def product(left, right, contract):
    return lax.dot_general(
        left, right, (((contract[0],), (contract[1],)), ((), ())), preferred_element_type=jnp.float32
    )


def probabilities_of(query, key, allowed):
    scores = jnp.where(allowed, product(key, query, (1, 1)) * HEAD_DIM ** (-0.5), -1e30)
    exponent = jnp.exp(scores - jnp.max(scores, axis=0, keepdims=True))
    return exponent * (1.0 / jnp.sum(exponent, axis=0, keepdims=True))


def attend_kernel(query_ref, key_ref, value_ref, column_ref, row_ref, mixed_ref):
    allowed = column_ref[0] == row_ref[0]
    parts = []
    for head in range(2):
        cols = slice(head * HEAD_DIM, (head + 1) * HEAD_DIM)
        probs = probabilities_of(query_ref[:, cols], key_ref[:, cols], allowed)
        mixed = product(value_ref[:, cols], probs.astype(jnp.bfloat16), (0, 0))
        parts.append(mixed.T)
    mixed_ref[...] = jnp.concatenate(parts, axis=1).astype(jnp.bfloat16)


def attend_back_kernel(
    query_ref, key_ref, value_ref, grad_ref, column_ref, row_ref, out_ref
):
    allowed = column_ref[0] == row_ref[0]
    scale = HEAD_DIM ** (-0.5)
    parts = []
    for head in range(2):
        cols = slice(head * HEAD_DIM, (head + 1) * HEAD_DIM)
        query, key, value = query_ref[:, cols], key_ref[:, cols], value_ref[:, cols]
        grad = grad_ref[:, cols]
        probs = probabilities_of(query, key, allowed)
        grad_value = product(probs.astype(jnp.bfloat16), grad, (1, 0))
        grad_probs = product(value, grad, (1, 1))
        centred = jnp.sum(probs * grad_probs, axis=0, keepdims=True)
        grad_scores = (probs * (grad_probs - centred)).astype(jnp.bfloat16)
        grad_key = product(grad_scores, query, (1, 0)) * scale
        grad_query = (product(key, grad_scores, (0, 0)) * scale).T
        parts.append((grad_query, grad_key, grad_value))
    for place in range(3):
        out_ref[place] = jnp.concatenate(
            [parts[0][place], parts[1][place]], axis=1
        ).astype(jnp.bfloat16)


def attention_specs(length, pairs):
    column = pl.BlockSpec((1, length, 1), lambda s, h: (s, 0, 0))
    row = pl.BlockSpec((1, 1, length), lambda s, h: (s, 0, 0))
    blocks = [
        pl.BlockSpec((length, PAIR), functools.partial(lambda first, s, h: (s, first + h), k * pairs))
        for k in range(3)
    ]
    return blocks, column, row


def attend(projected, segments):
    seqs, length = segments.shape
    width = projected.shape[1] // 3
    pairs = width // PAIR
    blocks, column, row = attention_specs(length, pairs)
    cells = seqs * (width // HEAD_DIM) * length * length
    return pl.pallas_call(
        attend_kernel,
        grid=(seqs, pairs),
        out_shape=jax.ShapeDtypeStruct((seqs * length, width), jnp.bfloat16),
        in_specs=[*blocks, column, row],
        out_specs=pl.BlockSpec((length, PAIR), lambda s, h: (s, h)),
        compiler_params=pltpu.CompilerParams(vmem_limit_bytes=VMEM_BYTES),
        cost_estimate=pl.CostEstimate(
            flops=cells * 4 * HEAD_DIM, bytes_accessed=8 * seqs * length * width, transcendentals=cells
        ),
    )(projected, projected, projected, segments[:, :, None], segments[:, None, :])


def attend_back(projected, grad_mixed, segments):
    seqs, length = segments.shape
    width = projected.shape[1] // 3
    pairs = width // PAIR
    blocks, column, row = attention_specs(length, pairs)
    cells = seqs * (width // HEAD_DIM) * length * length
    return pl.pallas_call(
        attend_back_kernel,
        grid=(seqs, pairs),
        out_shape=jax.ShapeDtypeStruct((3, seqs * length, width), jnp.bfloat16),
        in_specs=[*blocks, blocks[0], column, row],
        out_specs=pl.BlockSpec((3, length, PAIR), lambda s, h: (0, s, h)),
        compiler_params=pltpu.CompilerParams(vmem_limit_bytes=VMEM_BYTES),
        cost_estimate=pl.CostEstimate(
            flops=cells * 10 * HEAD_DIM, bytes_accessed=14 * seqs * length * width, transcendentals=cells
        ),
    )(projected, projected, projected, grad_mixed, segments[:, :, None], segments[:, None, :])


def to_sequences(array):
    n, me = lax.axis_size("seq"), lax.axis_index("seq")
    some, rows, width = array.shape[0] // n, array.shape[1], array.shape[2]
    own = lax.dynamic_slice_in_dim(array, me * some, some, 0)
    whole = jnp.zeros((some, n * rows, width), array.dtype)
    whole = lax.dynamic_update_slice_in_dim(whole, own, me * rows, 1)
    for step in range(1, n):
        there, source = lax.rem(me + step, n), lax.rem(me + n - step, n)
        sent = lax.dynamic_slice_in_dim(array, there * some, some, 0)
        came = lax.ppermute(sent, "seq", [(i, (i + step) % n) for i in range(n)])
        whole = lax.dynamic_update_slice_in_dim(whole, came, source * rows, 1)
    return whole


def to_positions(array):
    n, me = lax.axis_size("seq"), lax.axis_index("seq")
    some, rows, width = array.shape[0], array.shape[1] // n, array.shape[2]
    own = lax.dynamic_slice_in_dim(array, me * rows, rows, 1)
    whole = jnp.zeros((n * some, rows, width), array.dtype)
    whole = lax.dynamic_update_slice_in_dim(whole, own, me * some, 0)
    for step in range(1, n):
        there, source = lax.rem(me + step, n), lax.rem(me + n - step, n)
        sent = lax.dynamic_slice_in_dim(array, there * rows, rows, 1)
        came = lax.ppermute(sent, "seq", [(i, (i + step) % n) for i in range(n)])
        whole = lax.dynamic_update_slice_in_dim(whole, came, source * some, 0)
    return whole


def packed_columns(vectors, rows):
    columns = jnp.concatenate([v.reshape(rows, -1) for v in vectors], axis=1)
    return jnp.pad(columns, ((0, 0), (0, PAD - columns.shape[1])))


def unpacked_columns(columns, sizes):
    rows, start, vectors = columns.shape[0], 0, []
    for size in sizes:
        wide = size // rows
        vectors.append(columns[:, start : start + wide].reshape(size))
        start += wide
    return vectors


def gathered(weight):
    return lax.all_gather(weight, ("fsdp", "seq"), axis=0, tiled=True)


def scattered(grad):
    return lax.psum_scatter(grad, ("fsdp", "seq"), scatter_dimension=0, tiled=True)


def shards(
    tokens,
    lengths,
    cotangent,
    project_weight,
    project_bias,
    output_weight,
    output_bias,
    first_gain,
    first_shift,
    expand_weight,
    expand_bias,
    reduce_weight,
    reduce_bias,
    second_gain,
    second_shift,
):
    model_width = tokens.shape[2]
    rows_own = project_weight.shape[0]
    devices = model_width // rows_own
    own_vectors = (
        project_bias, output_bias, first_gain, first_shift,
        expand_bias, reduce_bias, second_gain, second_shift,
    )
    sizes = [v.shape[0] * devices for v in own_vectors]
    first_pack = gathered(
        jnp.concatenate([project_weight, packed_columns(own_vectors, rows_own)], axis=1)
    )
    out_full = gathered(output_weight)
    expand_full = gathered(expand_weight)
    reduce_full = gathered(reduce_weight)
    inputs = to_sequences(tokens)
    grads_out = to_sequences(cotangent)
    proj_full = first_pack[:, : 3 * model_width]
    pbias, obias, gain_one, shift_one, ebias, rbias, gain_two, shift_two = (
        v.astype(jnp.float32) for v in unpacked_columns(first_pack[:, 3 * model_width :], sizes)
    )
    seqs_here, length, _ = inputs.shape
    own_lengths = lax.dynamic_slice_in_dim(
        lengths, lax.axis_index("seq") * seqs_here, seqs_here, 0
    )
    positions = jnp.arange(length, dtype=jnp.int32)
    doc_ends = jnp.cumsum(own_lengths, axis=1)
    segments = jnp.sum(
        (positions[None, :, None] >= doc_ends[:, None, :]).astype(jnp.int32), axis=2
    )
    flattened = inputs.reshape(-1, model_width)
    full_bias = jnp.concatenate(
        [pbias[:model_width], jnp.zeros((model_width,), jnp.float32), pbias[model_width:]]
    )
    projected = (
        jnp.dot(flattened, proj_full, preferred_element_type=jnp.float32) + full_bias
    ).astype(jnp.bfloat16)
    mixed_flat = attend(projected, segments)
    attention = jnp.dot(mixed_flat, out_full, preferred_element_type=jnp.float32) + obias
    residual_one = flattened.astype(jnp.float32) + attention
    first_norm = layer_norm(residual_one, gain_one, shift_one)
    first_low = first_norm.astype(jnp.bfloat16)
    inner_pre = jnp.dot(first_low, expand_full, preferred_element_type=jnp.float32) + ebias
    hidden = (inner_pre * normal_cdf(inner_pre)).astype(jnp.bfloat16)
    branch_out = jnp.dot(hidden, reduce_full, preferred_element_type=jnp.float32) + rbias
    residual_two = first_norm + branch_out
    result = layer_norm(residual_two, gain_two, shift_two).astype(jnp.bfloat16)
    activations = to_positions(result.reshape(inputs.shape))

    grad_result = grads_out.reshape(-1, model_width).astype(jnp.float32)
    norm_two_pull = jax.vjp(layer_norm, residual_two, gain_two, shift_two)[1]
    grad_residual_two, grad_gain_two, grad_shift_two = norm_two_pull(grad_result)
    grad_branch = grad_residual_two.astype(jnp.bfloat16)
    grad_reduce = product(hidden, grad_branch, (0, 0)).astype(jnp.bfloat16)
    grad_reduce, grad_branch = lax.optimization_barrier((grad_reduce, grad_branch))
    reduce_grad = scattered(grad_reduce).astype(jnp.float32)
    grad_rbias = jnp.sum(grad_branch.astype(jnp.float32), axis=0)
    grad_hidden = product(grad_branch, reduce_full, (1, 1))
    grad_inner = (gelu_slope(inner_pre) * grad_hidden).astype(jnp.bfloat16)
    grad_ebias = jnp.sum(grad_inner.astype(jnp.float32), axis=0)
    grad_expand = product(first_low, grad_inner, (0, 0)).astype(jnp.bfloat16)
    grad_expand, grad_inner = lax.optimization_barrier((grad_expand, grad_inner))
    expand_grad = scattered(grad_expand).astype(jnp.float32)
    grad_first = grad_residual_two + product(grad_inner, expand_full, (1, 1))
    norm_one_pull = jax.vjp(layer_norm, residual_one, gain_one, shift_one)[1]
    grad_residual_one, grad_gain_one, grad_shift_one = norm_one_pull(grad_first)
    grad_attention = grad_residual_one.astype(jnp.bfloat16)
    grad_outw = product(mixed_flat, grad_attention, (0, 0))
    grad_obias = jnp.sum(grad_attention.astype(jnp.float32), axis=0)
    early_vectors = (
        grad_obias, grad_gain_one, grad_shift_one,
        grad_ebias, grad_rbias, grad_gain_two, grad_shift_two,
    )
    grad_mixed = product(grad_attention, out_full, (1, 1)).astype(jnp.bfloat16)
    back = attend_back(projected, grad_mixed, segments)
    grad_projected = jnp.concatenate([back[0], back[1], back[2]], axis=1)
    grad_project = product(flattened, grad_projected, (0, 0))
    grad_column_sums = jnp.sum(grad_projected.astype(jnp.float32), axis=0)
    grad_pbias = jnp.concatenate(
        [grad_column_sums[:model_width], grad_column_sums[2 * model_width :]]
    )
    late = jnp.concatenate(
        [grad_project, grad_outw, packed_columns((grad_pbias, *early_vectors), model_width)],
        axis=1,
    ).astype(jnp.bfloat16)
    late, grad_projected = lax.optimization_barrier((late, grad_projected))
    late_pack = scattered(late).astype(jnp.float32)
    project_grad = late_pack[:, : 3 * model_width]
    output_grad = late_pack[:, 3 * model_width : 4 * model_width]
    (
        projbias_grad,
        outbias_grad,
        firstgain_grad,
        firstshift_grad,
        expbias_grad,
        redbias_grad,
        secondgain_grad,
        secondshift_grad,
    ) = unpacked_columns(late_pack[:, 4 * model_width :], [v.shape[0] for v in own_vectors])
    grad_inputs = grad_residual_one + product(grad_projected, proj_full, (1, 1))
    input_grad = to_positions(
        grad_inputs.astype(jnp.bfloat16).reshape(inputs.shape)
    ).astype(jnp.float32)
    return (
        activations,
        input_grad,
        project_grad,
        projbias_grad,
        output_grad,
        outbias_grad,
        firstgain_grad,
        firstshift_grad,
        expand_grad,
        expbias_grad,
        reduce_grad,
        redbias_grad,
        secondgain_grad,
        secondshift_grad,
    )


def solution(mesh):
    in_specs = (
        P("fsdp", "seq", None),
        P("fsdp", None),
        P("fsdp", "seq", None),
        P(("fsdp", "seq"), None),
        P(("fsdp", "seq")),
        P(("fsdp", "seq"), None),
        P(("fsdp", "seq")),
        P(("fsdp", "seq")),
        P(("fsdp", "seq")),
        P(("fsdp", "seq"), None),
        P(("fsdp", "seq")),
        P(("fsdp", "seq"), None),
        P(("fsdp", "seq")),
        P(("fsdp", "seq")),
        P(("fsdp", "seq")),
    )
    out_specs = (
        P("fsdp", "seq", None),
        P("fsdp", "seq", None),
        P(("fsdp", "seq"), None),
        P(("fsdp", "seq")),
        P(("fsdp", "seq"), None),
        P(("fsdp", "seq")),
        P(("fsdp", "seq")),
        P(("fsdp", "seq")),
        P(("fsdp", "seq"), None),
        P(("fsdp", "seq")),
        P(("fsdp", "seq"), None),
        P(("fsdp", "seq")),
        P(("fsdp", "seq")),
        P(("fsdp", "seq")),
    )
    return jax.shard_map(shards, mesh=mesh, in_specs=in_specs, out_specs=out_specs, check_vma=False)
```

time: 1420 us -> 738 us (0.52)
  waiting for transfers between devices: 952 us -> 490 us
  matrix products: 207 us -> 86.7 us
  blocking collectives: 84.8 us -> 0 us
  local copies, waits for them, and re-layouts: 110 us -> 43.2 us
  Pallas kernels: 0 us -> 49.2 us
  starting transfers between devices: 0.98 us -> 19 us
    reduce_scatter x5 -> x2, waiting for transfers between devices: 498 us -> 103 us  [scattered(): lax.psum_scatter(grad, ('fsdp', 'seq'), scatter_dimension=0, tiled=True)]
    all_gather x6 -> x4, waiting for transfers between devices: 326 us -> 163 us  [gathered(): return lax.all_gather(weight, ('fsdp', 'seq'), axis=0, tiled=True)]
    dot_general x25 -> x11, matrix products: 200 us -> 80.4 us  [the longest x8 55.4 us: product(): lax.dot_general(left, right, (((contract[0],), (contract[1],)), ((), ()))...]
    ppermute x0 -> x12, waiting for transfers between devices: none -> 115 us  [the longest x6 60.3 us: to_positions(): came = lax.ppermute(sent, 'seq', [(i, (i + step) % n) for i in range(n)])]
    unnamed x2 -> x0, blocking collectives: 84.8 us -> none
    pallas_call x0 -> x2, Pallas kernels: none -> 49.2 us  [the longest x1 29.3 us: attend_back(): pl.pallas_call(attend_back_kernel, grid=(seqs, pairs), out_shape=jax.Shap...]
    dynamic_slice x15 -> x5, local copies, waits for them, and re-layouts: 22 us -> 2.19 us  [the longest x2 1.92 us: to_sequences(): sent = lax.dynamic_slice_in_dim(array, there * some, some, 0)]
    unnamed x13 -> x8, waiting for transfers between devices: 128 us -> 109 us
  transfers between devices with their start and end apart: 12 -> 19, of which waited for: 12 -> 14; matrix products, arithmetic and copies ran while one was open for 12% -> 12% of each run, Pallas kernels for 0% -> 7%
where the time goes in v1:
time: 738 us; the launch traced here: 732 us
  waiting for transfers between devices  490 us (66%)
  matrix products  86.7 us (12%)
  Pallas kernels  49.2 us (7%)
  local copies, waits for them, and re-layouts  43.2 us (6%)
  other arithmetic  29 us (4%)
  starting transfers between devices  19 us (3%)
  between operations  15.1 us (2%)
    all_gather x4, waiting for transfers between devices, gathered(): return lax.all_gather(weight, ('fsdp', 'seq'), axis=0, tiled=True)  163 us
    unnamed x8, waiting for transfers between devices  109 us
    reduce_scatter x2, waiting for transfers between devices, scattered(): lax.psum_scatter(grad, ('fsdp', 'seq'), scatter_dimension=0, tiled=True)  103 us
    ppermute x6, waiting for transfers between devices, to_positions(): came = lax.ppermute(sent, 'seq', [(i, (i + step) % n) for i in range(n)])  60.3 us
    dot_general x8, matrix products, product(): lax.dot_general(left, right, (((contract[0],), (contract[1],)), ((), ()))...  55.4 us
    ppermute x6, waiting for transfers between devices, to_sequences(): came = lax.ppermute(sent, 'seq', [(i, (i + step) % n) for i in range(n)])  54.8 us
    pallas_call x1, Pallas kernels, attend_back(): pl.pallas_call(attend_back_kernel, grid=(seqs, pairs), out_shape=jax.Shap...  29.3 us
    pallas_call x1, Pallas kernels, attend(): pl.pallas_call(attend_kernel, grid=(seqs, pairs), out_shape=jax.ShapeDtyp...  19.9 us
  transfers between devices with their start and end apart: 19, of which 14 were waited for; matrix products, arithmetic and copies ran while one was open for 12% of the time, Pallas kernels for 7%

profile of v1, /device:TPU:0, one launch (start us, length us, event | category | flops | bytes accessed | tf_op | source)
XLA Modules:
  0.0 732.1 jit_solution(3258648814755402524)
XLA Ops:
  13.5 1.6 fusion.13
  18.2 3.0 collective-permute-start
  21.4 1.0 constant_dynamic-slice_fusion.1
  22.4 1.6 collective-permute-start.6
  24.0 1.4 collective-permute-start.1
  25.4 2.5 collective-permute-start.2
  29.0 5.6 collective-permute-done
  34.6 2.6 collective-permute-start.8
  37.2 1.8 constant_dynamic-update-slice_fusion.11
  39.0 5.6 collective-permute-done.6
  45.6 15.9 %collective-permute-done.1 = bf16[2,128,768]{2,1,0:T(8,128)(2,1)} collective-permute-done((bf16[2,128,768]{2,1,0:T(8,128)(2,1)S(1)}, bf16[2,128,768]{2,1,0:T(8,128)(2,1)}, u32[]{:S(2)}, u32[]{:S(2)}) %collective-permute-start.1) | collective-permute-done | bytes 393248 | tf_op jit(solution)/shard_map/ppermute | solution.py:138
  61.5 1.8 constant_dynamic-update-slice_fusion.10
  63.3 27.7 %collective-permute-done.7 = bf16[2,128,768]{2,1,0:T(8,128)(2,1)} collective-permute-done((bf16[2,128,768]{2,1,0:T(8,128)(2,1)}, bf16[2,128,768]{2,1,0:T(8,128)(2,1)}, u32[]{:S(2)}, u32[]{:S(2)}) %collective-permute-start.7) | collective-permute-done | bytes 393248 | tf_op jit(solution)/shard_map/ppermute | solution.py:138
  92.0 1.8 constant_dynamic-update-slice_fusion.9
  93.8 28.4 %all-gather.5.cloned.1.call-done = bf16[768,2432]{1,0:T(8,128)(2,1)} async-done(((bf16[24,2432]{1,0:T(8,128)(2,1)}), bf16[768,2432]{1,0:T(8,128)(2,1)}) %all-gather.5.cloned.1.call-update) | async-done | bytes 3735568 | tf_op jit(solution)/shard_map/all_gather | solution.py:172
  122.2 1.0 slice_convert_fusion
  124.7 2.5 convert_reduce_fusion.1
  127.3 6.3 add_convert_fusion.query_ref.key_ref.value_ref
  133.6 19.9 %shard_map.254 = bf16[1024,768]{1,0:T(8,128)(2,1)S(1)} custom-call(bf16[1024,2304]{1,0:T(8,128)(2,1)S(1)} %add_convert_fusion.query_ref.key_ref.value_ref, bf16[1024,2304]{1,0:T(8,128)(2,1)S(1)} %add_convert_fusion.query_ref.key_ref.value_ref, bf16[1024,2304]{1,0:T(8,128)(2,1)S(1)} %add_convert_fusion.query_ref.key_ref.value_ref, ...), custom_call_target="tpu_custom_call" | custom-call | flops 1610612736 | bytes 6291456 | tf_op jit(solution)/shard_map/pallas_call | solution.py:97
  153.5 2.1 copy-done.2
  155.6 22.4 %all-gather.7.cloned.1.call-done = bf16[768,768]{1,0:T(8,128)(2,1)} async-done(((bf16[24,768]{1,0:T(8,128)(2,1)}), bf16[768,768]{1,0:T(8,128)(2,1)}) %all-gather.7.cloned.1.call-update) | async-done | bytes 1179664 | tf_op jit(solution)/shard_map/all_gather | solution.py:172
  178.1 3.3 fusion.26
  181.4 1.6 copy-done.5
  183.6 59.8 %all-gather.9.cloned.1.call-done = bf16[768,3072]{1,0:T(8,128)(2,1)} async-done(((bf16[24,3072]{1,0:T(8,128)(2,1)}), bf16[768,3072]{1,0:T(8,128)(2,1)}) %all-gather.9.cloned.1.call-update) | async-done | bytes 4718608 | tf_op jit(solution)/shard_map/all_gather | solution.py:172
  243.4 12.5 %multiply_convert_fusion.1 = (bf16[1024,3072]{1,0:T(8,128)(2,1)}, f32[1024,3072]{1,0:T(8,128)}) fusion(f32[3072]{0:T(1024)S(1)} %reshape.294, bf16[768,3072]{1,0:T(8,128)(2,1)} %all-gather.9.cloned.1.call-done, f32[1024,768]{1,0:T(8,128)} %copy-done.5, f32[768]{0:T(1024)S(1)} %get-tuple-element.33, f32[768]{0:T(1024)S(1)} %get-tuple-element.34, ...), kind=kOutput, calls=%fused_computation.1 | convolution fusion | flops 4854644736 | bytes 26765312 | tf_op jit(solution)/shard_map/dot_general | solution.py:237
  255.9 52.6 %all-gather.11.cloned.1.call-done = bf16[3072,768]{1,0:T(8,128)(2,1)} async-done(((bf16[96,768]{1,0:T(8,128)(2,1)}), bf16[3072,768]{1,0:T(8,128)(2,1)}) %all-gather.11.cloned.1.call-update) | async-done | bytes 4718608 | tf_op jit(solution)/shard_map/all_gather | solution.py:172
  308.5 9.3 %fusion.27 = (f32[1024]{0:T(1024)S(1)}, f32[1024,768]{1,0:T(8,128)S(1)}) fusion(f32[768]{0:T(1024)S(1)} %get-tuple-element.32, bf16[1024,3072]{1,0:T(8,128)(2,1)} %get-tuple-element.77, bf16[3072,768]{1,0:T(8,128)(2,1)} %all-gather.11.cloned.1.call-done, f32[768]{0:T(1024)S(1)} %get-tuple-element.33, f32[768]{0:T(1024)S(1)} %get-tuple-element.34, ...), kind=kOutput, calls=%fused_computation.108 | convolution fusion | flops 4837342208 | bytes 17323008 | tf_op jit(solution)/shard_map/dot_general | solution.py:239
  319.2 1.2 fusion.5
  320.5 2.6 fusion.23
  323.1 1.6 copy-done.10
  325.0 1.2 copy-done.11
  326.1 7.1 convolution_convert_fusion.1
  333.2 12.4 %fusion.28 = (bf16[3072]{0:T(1024)(128)(2,1)S(1)}, bf16[1024,3072]{1,0:T(8,128)(2,1)S(1)}) fusion(bf16[1024,768]{1,0:T(8,128)(2,1)} %copy-done.11, bf16[3072,768]{1,0:T(8,128)(2,1)} %all-gather.11.cloned.1.call-done, f32[1024,3072]{1,0:T(8,128)} %get-tuple-element.78, f32[3072]{0:T(1024)S(1)} %reshape.294), kind=kOutput, calls=%fused_computation.109 | convolution fusion | flops 4869583872 | bytes 25184256 | tf_op jit(solution)/shard_map/dot_general | solution.py:35
  345.6 2.7 copy-done.21
  348.3 8.1 %convolution_convert_fusion = bf16[768,3072]{1,0:T(8,128)(2,1)} fusion(bf16[1024,3072]{1,0:T(8,128)(2,1)S(1)} %get-tuple-element.21, f32[1024,768]{1,0:T(8,128)S(1)} %copy-done.6, f32[768]{0:T(1024)S(1)} %get-tuple-element.33, f32[768]{0:T(1024)S(1)} %get-tuple-element.34, f32[1024]{0:T(1024)S(1)} %fusion.15, f32[1024]{0:T(1024)S(1)} %broadcast_multiply_fusion.1), kind=kOutput, calls=%fused_computation.6 | convolution fusion | flops 4838129664 | bytes 14170112 | tf_op jit(solution)/shard_map/dot_general | solution.py:35
  356.4 1.7 reduce.5
  358.3 11.4 %multiply_reduce_fusion = (bf16[768]{0:T(1024)(128)(2,1)S(1)}, f32[1024]{0:T(1024)S(1)}, bf16[768]{0:T(1024)(128)(2,1)S(1)}, f32[1024,768]{1,0:T(8,128)S(1)}) fusion(f32[1024,768]{1,0:T(8,128)} %copy-done.5, f32[1024]{0:T(1024)S(1)} %fusion.15, f32[1024]{0:T(1024)S(1)} %broadcast_multiply_fusion.1, f32[768]{0:T(1024)S(1)} %get-tuple-element.34, ...), kind=kOutput, calls=%fused_computation.20 | convolution fusion | flops 4839699456 | bytes 20469760 | tf_op jit(solution)/shard_map/dot_general | solution.py:35
  369.8 1.4 fusion.22
  371.6 1.3 copy-done.8
  372.9 1.2 copy-done.13
  374.1 1.4 convolution_convert_fusion.3.grad_ref
  375.8 29.3 %shard_map.255 = bf16[3,1024,768]{2,1,0:T(8,128)(2,1)S(1)} custom-call(bf16[1024,2304]{1,0:T(8,128)(2,1)S(1)} %bitcast.43, bf16[1024,2304]{1,0:T(8,128)(2,1)S(1)} %bitcast.43, bf16[1024,2304]{1,0:T(8,128)(2,1)S(1)} %bitcast.43, bf16[1024,768]{1,0:T(8,128)(2,1)S(1)} %convolution_convert_fusion.3.grad_ref, s32[2,512,1]{2,1,0:T(8,128)S(1)} %copy.109.column_ref, ...), custom_call_target="tpu_custom_call" | custom-call | flops 4026531840 | bytes 11010048 | tf_op jit(solution)/shard_map/pallas_call | solution.py:116
  405.5 2.6 fusion.21
  409.5 1.7 reduce.4
  412.3 2.2 concatenate.30
  414.5 3.0 convolution_convert_fusion.4
  417.7 4.4 convolution_convert_fusion.2
  422.1 2.6 fusion.1
  424.8 1.9 copy-done.9
  426.6 7.6 %add_convert_fusion.1 = bf16[1024,768]{1,0:T(8,128)(2,1)S(1)} fusion(f32[1024,768]{1,0:T(8,128)S(1)} %copy-done.9, f32[1024]{0:T(1024)S(1)} %negate_multiply_fusion, bf16[1024,2304]{1,0:T(8,128)(2,1)} %get-tuple-element.22, bf16[768,2432]{1,0:T(8,128)(2,1)} %all-gather.5.cloned.1.call-done), kind=kOutput, calls=%fused_computation.19 | convolution fusion | flops 3626237952 | bytes 12980224 | tf_op jit(solution)/shard_map/dot_general | solution.py:35
  434.5 2.0 collective-permute-start.9
  436.8 2.4 collective-permute-start.11
  439.6 2.2 collective-permute-start.4
  441.8 9.4 %collective-permute-done.9 = bf16[2,128,768]{2,1,0:T(8,128)(2,1)S(1)} collective-permute-done((bf16[2,128,768]{2,1,0:T(8,128)(2,1)S(1)}, bf16[2,128,768]{2,1,0:T(8,128)(2,1)S(1)}, u32[]{:S(2)}, u32[]{:S(2)}) %collective-permute-start.9) | collective-permute-done | bytes 393248 | tf_op jit(solution)/shard_map/ppermute | solution.py:152
  451.4 16.5 %collective-permute-done.10 = bf16[2,128,768]{2,1,0:T(8,128)(2,1)S(1)} collective-permute-done((bf16[2,128,768]{2,1,0:T(8,128)(2,1)S(1)}, bf16[2,128,768]{2,1,0:T(8,128)(2,1)S(1)}, u32[]{:S(2)}, u32[]{:S(2)}) %collective-permute-start.10) | collective-permute-done | bytes 393248 | tf_op jit(solution)/shard_map/ppermute | solution.py:152
  468.0 1.9 convert_element_type.186
  469.9 9.0 %collective-permute-done.3 = bf16[2,128,768]{2,1,0:T(8,128)(2,1)S(1)} collective-permute-done((bf16[2,128,768]{2,1,0:T(8,128)(2,1)S(1)}, bf16[2,128,768]{2,1,0:T(8,128)(2,1)S(1)}, u32[]{:S(2)}, u32[]{:S(2)}) %collective-permute-start.3) | collective-permute-done | bytes 393248 | tf_op jit(solution)/shard_map/ppermute | solution.py:152
  479.0 25.3 %collective-permute-done.4 = bf16[2,128,768]{2,1,0:T(8,128)(2,1)S(1)} collective-permute-done((bf16[2,128,768]{2,1,0:T(8,128)(2,1)S(1)}, bf16[2,128,768]{2,1,0:T(8,128)(2,1)S(1)}, u32[]{:S(2)}, u32[]{:S(2)}) %collective-permute-start.4) | collective-permute-done | bytes 393248 | tf_op jit(solution)/shard_map/ppermute | solution.py:152
  504.5 1.8 convert_element_type.188
  506.3 102.6 %reduce-scatter.8.cloned.1.call-done = bf16[96,768]{1,0:T(8,128)(2,1)} async-done(((bf16[3072,768]{1,0:T(8,128)(2,1)}), bf16[96,768]{1,0:T(8,128)(2,1)}) %reduce-scatter.8.cloned.1.call-update) | async-done | bytes 147472 | tf_op jit(solution)/shard_map/reduce_scatter | solution.py:176
  608.9 1.6 convert_element_type.189
  610.5 107.0 %reduce-scatter.10.cloned.1.call-done = bf16[24,3200]{1,0:T(8,128)(2,1)} async-done(((bf16[768,3200]{1,0:T(8,128)(2,1)}), bf16[24,3200]{1,0:T(8,128)(2,1)}) %reduce-scatter.10.cloned.1.call-update) | async-done | bytes 153616
  722.0 1.6 slice.170
  723.6 1.4 slice.172
  (142 shorter events, 25.8 us)
Async XLA Ops:
  7.2 21.1 %copy-start = (s32[8,26]{1,0:T(8,128)S(1)}, s32[8,26]{1,0:T(8,128)}, u32[]{:S(2)}) copy-start(s32[8,26]{1,0:T(8,128)} %param.16) | copy-start | bytes 2500
  7.2 10.1 %copy-start.14 = (bf16[8,128,768]{2,1,0:T(8,128)(2,1)S(1)}, bf16[8,128,768]{2,1,0:T(8,128)(2,1)}, u32[]{:S(2)}) copy-start(bf16[8,128,768]{2,1,0:T(8,128)(2,1)} %param.15) | copy-start | bytes 4718596
  7.2 115.0 %all-gather.5.cloned.1.call-start = ((), (), s32[]{:S(2)}) async-start(), calls=%async_computation.3 | async-start | bytes 3852288 | tf_op jit(solution)/shard_map/all_gather | solution.py:172
  15.1 163.0 %all-gather.7.cloned.1.call-start = ((), (), s32[]{:S(2)}) async-start(), calls=%async_computation.4 | async-start | bytes 1216512 | tf_op jit(solution)/shard_map/all_gather | solution.py:172
  15.8 227.6 %all-gather.9.cloned.1.call-start = ((), (), s32[]{:S(2)}) async-start(), calls=%async_computation.5 | async-start | bytes 4866048 | tf_op jit(solution)/shard_map/all_gather | solution.py:172
  16.5 291.9 %all-gather.11.cloned.1.call-start = ((), (), s32[]{:S(2)}) async-start(), calls=%async_computation.6 | async-start | bytes 4866048 | tf_op jit(solution)/shard_map/all_gather | solution.py:172
  17.1 487.3 %reduce-scatter.6.cloned.1.call-start = ((), (), s32[]{:S(2)}) async-start(), calls=%async_computation.7 | async-start | bytes 4866048 | tf_op jit(solution)/shard_map/reduce_scatter | solution.py:176
  17.2 4.2 copy-start.15
  18.2 4.2 copy-start.17
  18.2 16.4 %collective-permute-start = (bf16[2,128,768]{2,1,0:T(8,128)(2,1)}, bf16[2,128,768]{2,1,0:T(8,128)(2,1)}, u32[]{:S(2)}, u32[]{:S(2)}) collective-permute-start(bf16[2,128,768]{2,1,0:T(8,128)(2,1)} %get-tuple-element.68), channel_id=1, source_target_pairs={{0,1},{1,2},{2,3},{3,0},{4,5},{5,6},{6,7},{7,4},{8,9},{9,10},{10,1... | collective-permute-start | bytes 1179656 | tf_op jit(solution)/shard_map/ppermute | solution.py:138
  22.4 22.1 %collective-permute-start.6 = (bf16[2,128,768]{2,1,0:T(8,128)(2,1)}, bf16[2,128,768]{2,1,0:T(8,128)(2,1)}, u32[]{:S(2)}, u32[]{:S(2)}) collective-permute-start(bf16[2,128,768]{2,1,0:T(8,128)(2,1)} %get-tuple-element.60), channel_id=1, source_target_pairs={{0,1},{1,2},{2,3},{3,0},{4,5},{5,6},{6,7},{7,4},{8,9},{9,10},{10,1... | collective-permute-start | bytes 1179656 | tf_op jit(solution)/shard_map/ppermute | solution.py:138
  24.0 37.5 %collective-permute-start.1 = (bf16[2,128,768]{2,1,0:T(8,128)(2,1)S(1)}, bf16[2,128,768]{2,1,0:T(8,128)(2,1)}, u32[]{:S(2)}, u32[]{:S(2)}) collective-permute-start(bf16[2,128,768]{2,1,0:T(8,128)(2,1)S(1)} %get-tuple-element.70), channel_id=1, source_target_pairs={{0,2},{1,3},{2,0},{3,1},{4,6},{5,7},{6,4},{7,5},{8,10},{9,11},{10,... | collective-permute-start | bytes 1179656 | tf_op jit(solution)/shard_map/ppermute | solution.py:138
  25.4 66.6 %collective-permute-start.2 = (bf16[2,128,768]{2,1,0:T(8,128)(2,1)S(1)}, bf16[2,128,768]{2,1,0:T(8,128)(2,1)}, u32[]{:S(2)}, u32[]{:S(2)}) collective-permute-start(bf16[2,128,768]{2,1,0:T(8,128)(2,1)S(1)} %get-tuple-element.67), channel_id=1, source_target_pairs={{0,3},{1,0},{2,1},{3,2},{4,7},{5,4},{6,5},{7,6},{8,11},{9,8},{10,9... | collective-permute-start | bytes 1179656 | tf_op jit(solution)/shard_map/ppermute | solution.py:138
  27.9 63.0 %collective-permute-start.7 = (bf16[2,128,768]{2,1,0:T(8,128)(2,1)}, bf16[2,128,768]{2,1,0:T(8,128)(2,1)}, u32[]{:S(2)}, u32[]{:S(2)}) collective-permute-start(bf16[2,128,768]{2,1,0:T(8,128)(2,1)} %get-tuple-element.62), channel_id=1, source_target_pairs={{0,2},{1,3},{2,0},{3,1},{4,6},{5,7},{6,4},{7,5},{8,10},{9,11},{10,... | collective-permute-start | bytes 1179656 | tf_op jit(solution)/shard_map/ppermute | solution.py:138
  34.6 59.2 %collective-permute-start.8 = (bf16[2,128,768]{2,1,0:T(8,128)(2,1)S(1)}, bf16[2,128,768]{2,1,0:T(8,128)(2,1)S(1)}, u32[]{:S(2)}, u32[]{:S(2)}) collective-permute-start(bf16[2,128,768]{2,1,0:T(8,128)(2,1)S(1)} %get-tuple-element.59), channel_id=1, source_target_pairs={{0,3},{1,0},{2,1},{3,2},{4,7},{5,4},{6,5},{7,6},{8,11},{9,8},{10,9... | collective-permute-start | bytes 1179656 | tf_op jit(solution)/shard_map/ppermute | solution.py:138
  93.8 33.5 %copy-start.3 = (bf16[2,512,768]{2,1,0:T(8,128)(2,1)}, bf16[2,512,768]{2,1,0:T(8,128)(2,1)S(1)}, u32[]{:S(2)}) copy-start(bf16[2,512,768]{2,1,0:T(8,128)(2,1)S(1)} %constant_dynamic-update-slice_fusion.2) | copy-start | bytes 4718596
  153.5 2.2 copy-start.2
  181.4 1.7 copy-start.5
  317.8 1.4 copy-start.4
  320.4 5.7 slice-start.4
  320.4 5.7 slice-start.5
  323.1 1.6 copy-start.10
  325.0 1.2 copy-start.11
  333.2 15.0 %copy-start.6 = (f32[1024,768]{1,0:T(8,128)S(1)}, f32[1024,768]{1,0:T(8,128)}, u32[]{:S(2)}) copy-start(f32[1024,768]{1,0:T(8,128)} %copy-done.5) | copy-start | bytes 9437188
  345.6 2.7 copy-start.21
  356.3 252.6 %reduce-scatter.8.cloned.1.call-start = ((), (), s32[]{:S(2)}) async-start(), calls=%async_computation.8 | async-start | bytes 4866048 | tf_op jit(solution)/shard_map/reduce_scatter | solution.py:176
  358.3 359.3 %reduce-scatter.10.cloned.1.call-start = ((), (), s32[]{:S(2)}) async-start(), calls=%async_computation.9 | async-start | bytes 5068800
  358.3 11.5 %copy-start.7 = (f32[1024,768]{1,0:T(8,128)S(1)}, f32[1024,768]{1,0:T(8,128)}, u32[]{:S(2)}) copy-start(f32[1024,768]{1,0:T(8,128)} %copy-done.5) | copy-start | bytes 9437188
  371.2 1.7 copy-start.8
  371.2 2.9 copy-start.20
  371.2 4.4 slice-start
  372.9 1.2 copy-start.13
  374.1 1.8 slice-start.1
  412.3 5.2 slice-start.2
  414.5 3.0 slice-start.3
  414.5 3.2 copy-start.18
  417.7 4.4 copy-start.19
  424.7 1.9 copy-start.9
  434.2 5.1 copy-start.12
  434.5 16.7 %collective-permute-start.9 = (bf16[2,128,768]{2,1,0:T(8,128)(2,1)S(1)}, bf16[2,128,768]{2,1,0:T(8,128)(2,1)S(1)}, u32[]{:S(2)}, u32[]{:S(2)}) collective-permute-start(bf16[2,128,768]{2,1,0:T(8,128)(2,1)S(1)} %get-tuple-element.57), channel_id=1, source_target_pairs={{0,1},{1,2},{2,3},{3,0},{4,5},{5,6},{6,7},{7,4},{8,9},{9,10},{10,1... | collective-permute-start | bytes 1179656 | tf_op jit(solution)/shard_map/ppermute | solution.py:152
  436.5 31.4 %collective-permute-start.10 = (bf16[2,128,768]{2,1,0:T(8,128)(2,1)S(1)}, bf16[2,128,768]{2,1,0:T(8,128)(2,1)S(1)}, u32[]{:S(2)}, u32[]{:S(2)}) collective-permute-start(bf16[2,128,768]{2,1,0:T(8,128)(2,1)S(1)} %get-tuple-element.56), channel_id=1, source_target_pairs={{0,2},{1,3},{2,0},{3,1},{4,6},{5,7},{6,4},{7,5},{8,10},{9,11},{10,... | collective-permute-start | bytes 1179656 | tf_op jit(solution)/shard_map/ppermute | solution.py:152
  436.8 31.1 %collective-permute-start.11 = (bf16[2,128,768]{2,1,0:T(8,128)(2,1)S(1)}, bf16[2,128,768]{2,1,0:T(8,128)(2,1)S(1)}, u32[]{:S(2)}, u32[]{:S(2)}) collective-permute-start(bf16[2,128,768]{2,1,0:T(8,128)(2,1)S(1)} %get-tuple-element.55), channel_id=1, source_target_pairs={{0,3},{1,0},{2,1},{3,2},{4,7},{5,4},{6,5},{7,6},{8,11},{9,8},{10,9... | collective-permute-start | bytes 1179656 | tf_op jit(solution)/shard_map/ppermute | solution.py:152
  439.5 39.5 %collective-permute-start.3 = (bf16[2,128,768]{2,1,0:T(8,128)(2,1)S(1)}, bf16[2,128,768]{2,1,0:T(8,128)(2,1)S(1)}, u32[]{:S(2)}, u32[]{:S(2)}) collective-permute-start(bf16[2,128,768]{2,1,0:T(8,128)(2,1)S(1)} %get-tuple-element.65), channel_id=1, source_target_pairs={{0,1},{1,2},{2,3},{3,0},{4,5},{5,6},{6,7},{7,4},{8,9},{9,10},{10,1... | collective-permute-start | bytes 1179656 | tf_op jit(solution)/shard_map/ppermute | solution.py:152
  439.6 64.8 %collective-permute-start.4 = (bf16[2,128,768]{2,1,0:T(8,128)(2,1)S(1)}, bf16[2,128,768]{2,1,0:T(8,128)(2,1)S(1)}, u32[]{:S(2)}, u32[]{:S(2)}) collective-permute-start(bf16[2,128,768]{2,1,0:T(8,128)(2,1)S(1)} %get-tuple-element.64), channel_id=1, source_target_pairs={{0,2},{1,3},{2,0},{3,1},{4,6},{5,7},{6,4},{7,5},{8,10},{9,11},{10,... | collective-permute-start | bytes 1179656 | tf_op jit(solution)/shard_map/ppermute | solution.py:152
  451.2 53.2 %collective-permute-start.5 = (bf16[2,128,768]{2,1,0:T(8,128)(2,1)S(1)}, bf16[2,128,768]{2,1,0:T(8,128)(2,1)S(1)}, u32[]{:S(2)}, u32[]{:S(2)}) collective-permute-start(bf16[2,128,768]{2,1,0:T(8,128)(2,1)S(1)} %get-tuple-element.63), channel_id=1, source_target_pairs={{0,3},{1,0},{2,1},{3,2},{4,7},{5,4},{6,5},{7,6},{8,11},{9,8},{10,9... | collective-permute-start | bytes 1179656 | tf_op jit(solution)/shard_map/ppermute | solution.py:152
  468.0 257.0 %copy-start.1 = (s32[8,26]{1,0:T(8,128)S(1)}, s32[8,26]{1,0:T(8,128)}, u32[]{:S(2)}) copy-start(s32[8,26]{1,0:T(8,128)} %param.16) | copy-start | bytes 2500
  504.4 220.6 %copy-start.16 = (bf16[8,128,768]{2,1,0:T(8,128)(2,1)}, bf16[8,128,768]{2,1,0:T(8,128)(2,1)S(1)}, u32[]{:S(2)}) copy-start(bf16[8,128,768]{2,1,0:T(8,128)(2,1)S(1)} %constant_dynamic-update-slice_fusion.5) | copy-start | bytes 4718596
Sparse Core Ops, SparseCore 0:
  15.2 106.9 all-gather.4
  125.0 53.0 all-gather.6
  180.9 62.4 all-gather.8
  246.1 62.3 all-gather.10
  356.5 134.8 reduce-scatter.5
  497.6 111.2 reduce-scatter.7
  614.6 102.9 reduce-scatter.9
